TPU v7x, 128 devices: a whole 4x4x4 slice. The times are simulated.
128 devices in a mesh: blk: 16 (over z_lo, x, core), seq: 8 (over z_hi, y).
Axes of the slice: x: 4, y: 4, z: 4 (z_hi: 2, z_lo: 2; z = z_hi * 2 + z_lo), core: 2. Of those that a mesh axis runs over, the one named last changes fastest.
Arguments:
- row_inputs: bfloat16 [8192, 3072], P('blk'), may hold values from -6 to 6
- row_grads: bfloat16 [8192, 3072], P('blk'), may hold values from -3 to 3
- gate_prob: float32 [8192], P('blk'), may hold values from 0.05 to 1
- live_counts: int32 [16], P('blk'), may hold values from 1 to 512, as said below
- gate_weight: bfloat16 [3072, 8192], P(None, ('blk', 'seq')), may hold values from -0.109375 to 0.109375
- up_weight: bfloat16 [3072, 8192], P(None, ('blk', 'seq')), may hold values from -0.109375 to 0.109375
- down_weight: bfloat16 [8192, 3072], P(('blk', 'seq')), may hold values from -0.0625 to 0.0625
Outputs:
- input_grad: bfloat16 [8192, 3072], P(('blk', 'seq'))
- prob_grad: float32 [8192], P(('blk', 'seq'))
- gate_grad: bfloat16 [3072, 8192], P(None, ('blk', 'seq'))
- up_grad: bfloat16 [3072, 8192], P(None, ('blk', 'seq'))
- down_grad: bfloat16 [8192, 3072], P(('blk', 'seq'))
Inputs may be any that keep to these rules, and one draw needn't show every extreme that they name: live_counts[b] routed rows fill the first slots of group b; the others are padding; in every draw some group is full.
All inputs are finite; a program needn't handle non-finite values.
Results may differ from a plain program's by a relative error of at most 0.023.
Values may be sent and summed in bfloat16 or wider, within the bound.
A program may use at most 192 MiB of HBM per device.

v0:
```python
import jax
import jax.numpy as jnp
from jax import lax
from jax.sharding import PartitionSpec as P


def shifted(value, axis, by):
    count = lax.axis_size(axis)
    return lax.ppermute(value, axis, [(i, (i + by) % count) for i in range(count)])


def contract_rows(left, right):
    return lax.dot_general(
        left, right, (((0,), (0,)), ((), ())), preferred_element_type=jnp.float32
    )


def contract_cols(left, right):
    return lax.dot_general(
        left, right, (((1,), (1,)), ((), ())), preferred_element_type=jnp.float32
    )


def local_terms(inputs_rows, grads_rows, scaled_rows, weight_rows, live_rows, packed, unit_count):
    gate_up = jnp.dot(inputs_rows, packed[:, : 2 * unit_count], preferred_element_type=jnp.float32)
    gate_pre = gate_up[:, :unit_count]
    up_pre = gate_up[:, unit_count:]
    sigmoid_gate = jax.nn.sigmoid(gate_pre)
    activated = gate_pre * sigmoid_gate
    hidden = (activated * up_pre).astype(jnp.bfloat16)
    back_hidden = jnp.dot(
        grads_rows, packed[:, 2 * unit_count :], preferred_element_type=jnp.float32
    )
    weighted_back = weight_rows[:, None] * back_hidden
    gate_back = weighted_back * up_pre * sigmoid_gate * (1.0 + gate_pre * (1.0 - sigmoid_gate))
    both_back = jnp.concatenate([gate_back, weighted_back * activated], axis=1).astype(jnp.bfloat16)
    input_part = contract_cols(both_back, packed[:, : 2 * unit_count])
    prob_part = jnp.sum(live_rows[:, None] * hidden.astype(jnp.float32) * back_hidden, axis=1)
    down_term = contract_rows(hidden, scaled_rows)
    in_term = contract_rows(inputs_rows, both_back)
    return (in_term, down_term, input_part, prob_part)


def shards(row_inputs, row_grads, gate_prob, live_counts, gate_weight, up_weight, down_weight):
    row_count = row_inputs.shape[0]
    feat_width = row_inputs.shape[1]
    unit_count = gate_weight.shape[1]
    group_total = lax.axis_size("blk")
    position = lax.axis_index("blk")
    live_count = live_counts[0]
    live_mask = (jnp.arange(row_count, dtype=jnp.int32) < live_count).astype(jnp.float32)
    weight_rows = live_mask * gate_prob
    scaled_grads = (weight_rows[:, None] * row_grads.astype(jnp.float32)).astype(jnp.bfloat16)
    packed = jnp.concatenate([gate_weight, up_weight, down_weight.T], axis=1)

    def contribute(carried, current, slice_index):
        in_buffer, down_buffer, input_total, prob_total = carried
        in_sum, down_sum, input_step, prob_step = local_terms(
            row_inputs, row_grads, scaled_grads, weight_rows, live_mask, current, unit_count
        )
        in_buffer = lax.dynamic_update_index_in_dim(
            in_buffer, in_sum.astype(jnp.bfloat16), slice_index, 0
        )
        down_buffer = lax.dynamic_update_index_in_dim(
            down_buffer, down_sum.astype(jnp.bfloat16), slice_index, 0
        )
        return (in_buffer, down_buffer, input_total + input_step, prob_total + prob_step)

    carried = (
        jnp.zeros((group_total, feat_width, 2 * unit_count), jnp.bfloat16),
        jnp.zeros((group_total, unit_count, feat_width), jnp.bfloat16),
        jnp.zeros((row_count, feat_width), jnp.float32),
        jnp.zeros((row_count,), jnp.float32),
    )
    carried = contribute(carried, packed, position)
    running = jnp.zeros((3 * feat_width * unit_count,), jnp.float32)

    def one_turn(turn_index, loop_state):
        weights_now, inner, partial_sums = loop_state
        weights_now = shifted(weights_now, "blk", 1)
        inner = contribute(inner, weights_now, (position - turn_index) % group_total)
        return (weights_now, inner, partial_sums)

    weights_now, carried, running = lax.fori_loop(
        1, group_total, one_turn, (packed, carried, running)
    )
    in_buffer, down_buffer, input_total, prob_total = carried
    in_sums, down_sums = (
        lax.psum_scatter(in_buffer, "blk", scatter_dimension=0, tiled=True).astype(jnp.float32),
        lax.psum_scatter(down_buffer, "blk", scatter_dimension=0, tiled=True).astype(jnp.float32),
    )
    in_own = in_sums[0]
    down_own = down_sums[0]
    gate_grad = in_own[:, :unit_count].astype(jnp.bfloat16)
    up_grad = in_own[:, unit_count:].astype(jnp.bfloat16)
    down_grad = down_own.astype(jnp.bfloat16)
    input_share, prob_share = (
        lax.psum_scatter(
            input_total.astype(jnp.bfloat16), "seq", scatter_dimension=0, tiled=True
        ).astype(jnp.float32),
        lax.psum_scatter(
            prob_total.astype(jnp.bfloat16), "seq", scatter_dimension=0, tiled=True
        ).astype(jnp.float32),
    )
    return (input_share.astype(jnp.bfloat16), prob_share, gate_grad, up_grad, down_grad)


def solution(mesh):
    placed = (
        P("blk", None),
        P("blk", None),
        P("blk"),
        P("blk"),
        P(None, ("blk", "seq")),
        P(None, ("blk", "seq")),
        P(("blk", "seq"), None),
    )
    return jax.shard_map(
        shards,
        mesh=mesh,
        in_specs=placed,
        out_specs=(
            P(("blk", "seq"), None),
            P(("blk", "seq")),
            P(None, ("blk", "seq")),
            P(None, ("blk", "seq")),
            P(("blk", "seq"), None),
        ),
        check_vma=False,
    )
```

profile of v0, /device:TPU:32, one launch (start us, length us, event | category | flops | bytes accessed | tf_op | source)
XLA Modules:
  0.0 786.3 jit_solution(2385972239839603585)
XLA Ops:
  18.7 4.7 fusion.20
  23.4 6.1 broadcast_in_dim.43
  35.1 507.3 %while.24 = (s32[]{:T(128)}, bf16[3072,192]{0,1:T(8,128)(2,1)}, bf16[16,3072,128]{1,2,0:T(8,128)(2,1)}, bf16[16,64,3072]{2,1,0:T(8,128)(2,1)}, f32[512,3072]{1,0...) while((s32[]{:T(128)}, bf16[3072,192]{0,1:T(8,128)(2,1)}, ...), condition=%wide.region_3.4_spmd.clone, body=%wide.region_1.3_spmd.clone.sunk | while | flops 1613956096 | bytes 105658848 | solution.py:84
  36.0 17.2 %collective-permute-done = bf16[3072,192]{0,1:T(8,128)(2,1)} collective-permute-done((bf16[3072,192]{0,1:T(8,128)(2,1)}, bf16[3072,192]{0,1:T(8,128)(2,1)}, u32[]{:S(2)}, u32[]{:S(2)}) %collective-permute-start) | collective-permute-done | bytes 1179680 | tf_op jit(solution)/shard_map/while/body/eval_jaxpr/ppermute | solution.py:9
  69.8 17.2 %collective-permute-done = bf16[3072,192]{0,1:T(8,128)(2,1)} collective-permute-done((bf16[3072,192]{0,1:T(8,128)(2,1)}, bf16[3072,192]{0,1:T(8,128)(2,1)}, u32[]{:S(2)}, u32[]{:S(2)}) %collective-permute-start) | collective-permute-done | bytes 1179680 | tf_op jit(solution)/shard_map/while/body/eval_jaxpr/ppermute | solution.py:9
  103.6 17.2 %collective-permute-done = bf16[3072,192]{0,1:T(8,128)(2,1)} collective-permute-done((bf16[3072,192]{0,1:T(8,128)(2,1)}, bf16[3072,192]{0,1:T(8,128)(2,1)}, u32[]{:S(2)}, u32[]{:S(2)}) %collective-permute-start) | collective-permute-done | bytes 1179680 | tf_op jit(solution)/shard_map/while/body/eval_jaxpr/ppermute | solution.py:9
  134.0 2.6 copy-done
  137.4 17.2 %collective-permute-done = bf16[3072,192]{0,1:T(8,128)(2,1)} collective-permute-done((bf16[3072,192]{0,1:T(8,128)(2,1)}, bf16[3072,192]{0,1:T(8,128)(2,1)}, u32[]{:S(2)}, u32[]{:S(2)}) %collective-permute-start) | collective-permute-done | bytes 1179680 | tf_op jit(solution)/shard_map/while/body/eval_jaxpr/ppermute | solution.py:9
  171.2 17.2 %collective-permute-done = bf16[3072,192]{0,1:T(8,128)(2,1)} collective-permute-done((bf16[3072,192]{0,1:T(8,128)(2,1)}, bf16[3072,192]{0,1:T(8,128)(2,1)}, u32[]{:S(2)}, u32[]{:S(2)}) %collective-permute-start) | collective-permute-done | bytes 1179680 | tf_op jit(solution)/shard_map/while/body/eval_jaxpr/ppermute | solution.py:9
  205.0 17.2 %collective-permute-done = bf16[3072,192]{0,1:T(8,128)(2,1)} collective-permute-done((bf16[3072,192]{0,1:T(8,128)(2,1)}, bf16[3072,192]{0,1:T(8,128)(2,1)}, u32[]{:S(2)}, u32[]{:S(2)}) %collective-permute-start) | collective-permute-done | bytes 1179680 | tf_op jit(solution)/shard_map/while/body/eval_jaxpr/ppermute | solution.py:9
  238.8 17.2 %collective-permute-done = bf16[3072,192]{0,1:T(8,128)(2,1)} collective-permute-done((bf16[3072,192]{0,1:T(8,128)(2,1)}, bf16[3072,192]{0,1:T(8,128)(2,1)}, u32[]{:S(2)}, u32[]{:S(2)}) %collective-permute-start) | collective-permute-done | bytes 1179680 | tf_op jit(solution)/shard_map/while/body/eval_jaxpr/ppermute | solution.py:9
  272.6 17.2 %collective-permute-done = bf16[3072,192]{0,1:T(8,128)(2,1)} collective-permute-done((bf16[3072,192]{0,1:T(8,128)(2,1)}, bf16[3072,192]{0,1:T(8,128)(2,1)}, u32[]{:S(2)}, u32[]{:S(2)}) %collective-permute-start) | collective-permute-done | bytes 1179680 | tf_op jit(solution)/shard_map/while/body/eval_jaxpr/ppermute | solution.py:9
  306.4 17.2 %collective-permute-done = bf16[3072,192]{0,1:T(8,128)(2,1)} collective-permute-done((bf16[3072,192]{0,1:T(8,128)(2,1)}, bf16[3072,192]{0,1:T(8,128)(2,1)}, u32[]{:S(2)}, u32[]{:S(2)}) %collective-permute-start) | collective-permute-done | bytes 1179680 | tf_op jit(solution)/shard_map/while/body/eval_jaxpr/ppermute | solution.py:9
  340.3 17.2 %collective-permute-done = bf16[3072,192]{0,1:T(8,128)(2,1)} collective-permute-done((bf16[3072,192]{0,1:T(8,128)(2,1)}, bf16[3072,192]{0,1:T(8,128)(2,1)}, u32[]{:S(2)}, u32[]{:S(2)}) %collective-permute-start) | collective-permute-done | bytes 1179680 | tf_op jit(solution)/shard_map/while/body/eval_jaxpr/ppermute | solution.py:9
  374.1 17.2 %collective-permute-done = bf16[3072,192]{0,1:T(8,128)(2,1)} collective-permute-done((bf16[3072,192]{0,1:T(8,128)(2,1)}, bf16[3072,192]{0,1:T(8,128)(2,1)}, u32[]{:S(2)}, u32[]{:S(2)}) %collective-permute-start) | collective-permute-done | bytes 1179680 | tf_op jit(solution)/shard_map/while/body/eval_jaxpr/ppermute | solution.py:9
  407.9 17.2 %collective-permute-done = bf16[3072,192]{0,1:T(8,128)(2,1)} collective-permute-done((bf16[3072,192]{0,1:T(8,128)(2,1)}, bf16[3072,192]{0,1:T(8,128)(2,1)}, u32[]{:S(2)}, u32[]{:S(2)}) %collective-permute-start) | collective-permute-done | bytes 1179680 | tf_op jit(solution)/shard_map/while/body/eval_jaxpr/ppermute | solution.py:9
  441.7 17.2 %collective-permute-done = bf16[3072,192]{0,1:T(8,128)(2,1)} collective-permute-done((bf16[3072,192]{0,1:T(8,128)(2,1)}, bf16[3072,192]{0,1:T(8,128)(2,1)}, u32[]{:S(2)}, u32[]{:S(2)}) %collective-permute-start) | collective-permute-done | bytes 1179680 | tf_op jit(solution)/shard_map/while/body/eval_jaxpr/ppermute | solution.py:9
  475.6 17.2 %collective-permute-done = bf16[3072,192]{0,1:T(8,128)(2,1)} collective-permute-done((bf16[3072,192]{0,1:T(8,128)(2,1)}, bf16[3072,192]{0,1:T(8,128)(2,1)}, u32[]{:S(2)}, u32[]{:S(2)}) %collective-permute-start) | collective-permute-done | bytes 1179680 | tf_op jit(solution)/shard_map/while/body/eval_jaxpr/ppermute | solution.py:9
  509.4 17.2 %collective-permute-done = bf16[3072,192]{0,1:T(8,128)(2,1)} collective-permute-done((bf16[3072,192]{0,1:T(8,128)(2,1)}, bf16[3072,192]{0,1:T(8,128)(2,1)}, u32[]{:S(2)}, u32[]{:S(2)}) %collective-permute-start) | collective-permute-done | bytes 1179680 | tf_op jit(solution)/shard_map/while/body/eval_jaxpr/ppermute | solution.py:9
  542.5 5.0 convert_element_type.107
  549.5 24.6 %all-reduce = bf16[512]{0:T(512)(128)(2,1)S(1)} all-reduce(bf16[512]{0:T(512)(128)(2,1)S(1)} %convert_element_type.108), channel_id=3, replica_groups=mesh['blk'=16,'seq'=8] {'seq'}, use_global_device_ids=true, to_apply=%region_5.6.clone | all-reduce | flops 512 | bytes 2048
  574.6 49.1 %reduce-scatter.6.cloned.1.call-done = bf16[1,3072,128]{1,2,0:T(8,128)(2,1)} async-done(((bf16[16,3072,128]{1,2,0:T(8,128)(2,1)}), bf16[1,3072,128]{1,2,0:T(8,128)(2,1)}) %reduce-scatter.6.cloned.1.call-update) | async-done | bytes 786448 | tf_op jit(solution)/shard_map/reduce_scatter | solution.py:89
  625.8 81.7 %reduce-scatter.4.cloned.1.call-done = bf16[64,3072]{1,0:T(8,128)(2,1)} async-done(((bf16[512,3072]{1,0:T(8,128)(2,1)}), bf16[64,3072]{1,0:T(8,128)(2,1)}) %reduce-scatter.4.cloned.1.call-update) | async-done | bytes 393232 | tf_op jit(solution)/shard_map/reduce_scatter | solution.py:98
  707.5 72.3 %reduce-scatter.8.cloned.1.call-done = bf16[1,64,3072]{2,1,0:T(8,128)(2,1)} async-done(((bf16[16,64,3072]{2,1,0:T(8,128)(2,1)}), bf16[1,64,3072]{2,1,0:T(8,128)(2,1)}) %reduce-scatter.8.cloned.1.call-update) | async-done | bytes 393232 | tf_op jit(solution)/shard_map/reduce_scatter | solution.py:90
  (334 shorter events, 265.1 us)
Async XLA Ops:
  7.2 616.6 %reduce-scatter.6.cloned.1.call-start = ((), (), s32[]{:S(2)}) async-start(), calls=%async_computation.4 | async-start | bytes 13369344 | tf_op jit(solution)/shard_map/reduce_scatter | solution.py:89
  35.1 18.1 %collective-permute-start = (bf16[3072,192]{0,1:T(8,128)(2,1)}, bf16[3072,192]{0,1:T(8,128)(2,1)}, u32[]{:S(2)}, u32[]{:S(2)}) collective-permute-start(bf16[3072,192]{0,1:T(8,128)(2,1)} %get-tuple-element.462), channel_id=1, source_target_pairs={{0,8},{8,16},{16,24},{24,32},{32,40},{40,48},{48,56},{56,64},{64,7... | collective-permute-start | bytes 3538952 | tf_op jit(solution)/shard_map/while/body/eval_jaxpr/ppermute | solution.py:9
  69.0 18.1 %collective-permute-start = (bf16[3072,192]{0,1:T(8,128)(2,1)}, bf16[3072,192]{0,1:T(8,128)(2,1)}, u32[]{:S(2)}, u32[]{:S(2)}) collective-permute-start(bf16[3072,192]{0,1:T(8,128)(2,1)} %get-tuple-element.462), channel_id=1, source_target_pairs={{0,8},{8,16},{16,24},{24,32},{32,40},{40,48},{48,56},{56,64},{64,7... | collective-permute-start | bytes 3538952 | tf_op jit(solution)/shard_map/while/body/eval_jaxpr/ppermute | solution.py:9
  102.8 18.1 %collective-permute-start = (bf16[3072,192]{0,1:T(8,128)(2,1)}, bf16[3072,192]{0,1:T(8,128)(2,1)}, u32[]{:S(2)}, u32[]{:S(2)}) collective-permute-start(bf16[3072,192]{0,1:T(8,128)(2,1)} %get-tuple-element.462), channel_id=1, source_target_pairs={{0,8},{8,16},{16,24},{24,32},{32,40},{40,48},{48,56},{56,64},{64,7... | collective-permute-start | bytes 3538952 | tf_op jit(solution)/shard_map/while/body/eval_jaxpr/ppermute | solution.py:9
  102.8 20.4 %copy-start.6 = (bf16[512,3072]{1,0:T(8,128)(2,1)S(1)}, bf16[512,3072]{1,0:T(8,128)(2,1)}, u32[]{:S(2)}) copy-start(bf16[512,3072]{1,0:T(8,128)(2,1)} %get-tuple-element.484) | copy-start | bytes 9437188 | tf_op jit(solution)/shard_map/while
  136.6 18.1 %collective-permute-start = (bf16[3072,192]{0,1:T(8,128)(2,1)}, bf16[3072,192]{0,1:T(8,128)(2,1)}, u32[]{:S(2)}, u32[]{:S(2)}) collective-permute-start(bf16[3072,192]{0,1:T(8,128)(2,1)} %get-tuple-element.462), channel_id=1, source_target_pairs={{0,8},{8,16},{16,24},{24,32},{32,40},{40,48},{48,56},{56,64},{64,7... | collective-permute-start | bytes 3538952 | tf_op jit(solution)/shard_map/while/body/eval_jaxpr/ppermute | solution.py:9
  136.6 20.4 %copy-start.6 = (bf16[512,3072]{1,0:T(8,128)(2,1)S(1)}, bf16[512,3072]{1,0:T(8,128)(2,1)}, u32[]{:S(2)}) copy-start(bf16[512,3072]{1,0:T(8,128)(2,1)} %get-tuple-element.484) | copy-start | bytes 9437188 | tf_op jit(solution)/shard_map/while
  170.4 18.1 %collective-permute-start = (bf16[3072,192]{0,1:T(8,128)(2,1)}, bf16[3072,192]{0,1:T(8,128)(2,1)}, u32[]{:S(2)}, u32[]{:S(2)}) collective-permute-start(bf16[3072,192]{0,1:T(8,128)(2,1)} %get-tuple-element.462), channel_id=1, source_target_pairs={{0,8},{8,16},{16,24},{24,32},{32,40},{40,48},{48,56},{56,64},{64,7... | collective-permute-start | bytes 3538952 | tf_op jit(solution)/shard_map/while/body/eval_jaxpr/ppermute | solution.py:9
  204.2 18.1 %collective-permute-start = (bf16[3072,192]{0,1:T(8,128)(2,1)}, bf16[3072,192]{0,1:T(8,128)(2,1)}, u32[]{:S(2)}, u32[]{:S(2)}) collective-permute-start(bf16[3072,192]{0,1:T(8,128)(2,1)} %get-tuple-element.462), channel_id=1, source_target_pairs={{0,8},{8,16},{16,24},{24,32},{32,40},{40,48},{48,56},{56,64},{64,7... | collective-permute-start | bytes 3538952 | tf_op jit(solution)/shard_map/while/body/eval_jaxpr/ppermute | solution.py:9
  238.0 18.1 %collective-permute-start = (bf16[3072,192]{0,1:T(8,128)(2,1)}, bf16[3072,192]{0,1:T(8,128)(2,1)}, u32[]{:S(2)}, u32[]{:S(2)}) collective-permute-start(bf16[3072,192]{0,1:T(8,128)(2,1)} %get-tuple-element.462), channel_id=1, source_target_pairs={{0,8},{8,16},{16,24},{24,32},{32,40},{40,48},{48,56},{56,64},{64,7... | collective-permute-start | bytes 3538952 | tf_op jit(solution)/shard_map/while/body/eval_jaxpr/ppermute | solution.py:9
  238.0 20.4 %copy-start.6 = (bf16[512,3072]{1,0:T(8,128)(2,1)S(1)}, bf16[512,3072]{1,0:T(8,128)(2,1)}, u32[]{:S(2)}) copy-start(bf16[512,3072]{1,0:T(8,128)(2,1)} %get-tuple-element.484) | copy-start | bytes 9437188 | tf_op jit(solution)/shard_map/while
  271.8 18.1 %collective-permute-start = (bf16[3072,192]{0,1:T(8,128)(2,1)}, bf16[3072,192]{0,1:T(8,128)(2,1)}, u32[]{:S(2)}, u32[]{:S(2)}) collective-permute-start(bf16[3072,192]{0,1:T(8,128)(2,1)} %get-tuple-element.462), channel_id=1, source_target_pairs={{0,8},{8,16},{16,24},{24,32},{32,40},{40,48},{48,56},{56,64},{64,7... | collective-permute-start | bytes 3538952 | tf_op jit(solution)/shard_map/while/body/eval_jaxpr/ppermute | solution.py:9
  271.8 20.4 %copy-start.6 = (bf16[512,3072]{1,0:T(8,128)(2,1)S(1)}, bf16[512,3072]{1,0:T(8,128)(2,1)}, u32[]{:S(2)}) copy-start(bf16[512,3072]{1,0:T(8,128)(2,1)} %get-tuple-element.484) | copy-start | bytes 9437188 | tf_op jit(solution)/shard_map/while
  305.6 18.1 %collective-permute-start = (bf16[3072,192]{0,1:T(8,128)(2,1)}, bf16[3072,192]{0,1:T(8,128)(2,1)}, u32[]{:S(2)}, u32[]{:S(2)}) collective-permute-start(bf16[3072,192]{0,1:T(8,128)(2,1)} %get-tuple-element.462), channel_id=1, source_target_pairs={{0,8},{8,16},{16,24},{24,32},{32,40},{40,48},{48,56},{56,64},{64,7... | collective-permute-start | bytes 3538952 | tf_op jit(solution)/shard_map/while/body/eval_jaxpr/ppermute | solution.py:9
  339.5 18.1 %collective-permute-start = (bf16[3072,192]{0,1:T(8,128)(2,1)}, bf16[3072,192]{0,1:T(8,128)(2,1)}, u32[]{:S(2)}, u32[]{:S(2)}) collective-permute-start(bf16[3072,192]{0,1:T(8,128)(2,1)} %get-tuple-element.462), channel_id=1, source_target_pairs={{0,8},{8,16},{16,24},{24,32},{32,40},{40,48},{48,56},{56,64},{64,7... | collective-permute-start | bytes 3538952 | tf_op jit(solution)/shard_map/while/body/eval_jaxpr/ppermute | solution.py:9
  373.3 18.1 %collective-permute-start = (bf16[3072,192]{0,1:T(8,128)(2,1)}, bf16[3072,192]{0,1:T(8,128)(2,1)}, u32[]{:S(2)}, u32[]{:S(2)}) collective-permute-start(bf16[3072,192]{0,1:T(8,128)(2,1)} %get-tuple-element.462), channel_id=1, source_target_pairs={{0,8},{8,16},{16,24},{24,32},{32,40},{40,48},{48,56},{56,64},{64,7... | collective-permute-start | bytes 3538952 | tf_op jit(solution)/shard_map/while/body/eval_jaxpr/ppermute | solution.py:9
  407.1 18.1 %collective-permute-start = (bf16[3072,192]{0,1:T(8,128)(2,1)}, bf16[3072,192]{0,1:T(8,128)(2,1)}, u32[]{:S(2)}, u32[]{:S(2)}) collective-permute-start(bf16[3072,192]{0,1:T(8,128)(2,1)} %get-tuple-element.462), channel_id=1, source_target_pairs={{0,8},{8,16},{16,24},{24,32},{32,40},{40,48},{48,56},{56,64},{64,7... | collective-permute-start | bytes 3538952 | tf_op jit(solution)/shard_map/while/body/eval_jaxpr/ppermute | solution.py:9
  407.1 20.4 %copy-start.6 = (bf16[512,3072]{1,0:T(8,128)(2,1)S(1)}, bf16[512,3072]{1,0:T(8,128)(2,1)}, u32[]{:S(2)}) copy-start(bf16[512,3072]{1,0:T(8,128)(2,1)} %get-tuple-element.484) | copy-start | bytes 9437188 | tf_op jit(solution)/shard_map/while
  440.9 18.1 %collective-permute-start = (bf16[3072,192]{0,1:T(8,128)(2,1)}, bf16[3072,192]{0,1:T(8,128)(2,1)}, u32[]{:S(2)}, u32[]{:S(2)}) collective-permute-start(bf16[3072,192]{0,1:T(8,128)(2,1)} %get-tuple-element.462), channel_id=1, source_target_pairs={{0,8},{8,16},{16,24},{24,32},{32,40},{40,48},{48,56},{56,64},{64,7... | collective-permute-start | bytes 3538952 | tf_op jit(solution)/shard_map/while/body/eval_jaxpr/ppermute | solution.py:9
  440.9 20.4 %copy-start.6 = (bf16[512,3072]{1,0:T(8,128)(2,1)S(1)}, bf16[512,3072]{1,0:T(8,128)(2,1)}, u32[]{:S(2)}) copy-start(bf16[512,3072]{1,0:T(8,128)(2,1)} %get-tuple-element.484) | copy-start | bytes 9437188 | tf_op jit(solution)/shard_map/while
  474.8 18.1 %collective-permute-start = (bf16[3072,192]{0,1:T(8,128)(2,1)}, bf16[3072,192]{0,1:T(8,128)(2,1)}, u32[]{:S(2)}, u32[]{:S(2)}) collective-permute-start(bf16[3072,192]{0,1:T(8,128)(2,1)} %get-tuple-element.462), channel_id=1, source_target_pairs={{0,8},{8,16},{16,24},{24,32},{32,40},{40,48},{48,56},{56,64},{64,7... | collective-permute-start | bytes 3538952 | tf_op jit(solution)/shard_map/while/body/eval_jaxpr/ppermute | solution.py:9
  508.6 18.1 %collective-permute-start = (bf16[3072,192]{0,1:T(8,128)(2,1)}, bf16[3072,192]{0,1:T(8,128)(2,1)}, u32[]{:S(2)}, u32[]{:S(2)}) collective-permute-start(bf16[3072,192]{0,1:T(8,128)(2,1)} %get-tuple-element.462), channel_id=1, source_target_pairs={{0,8},{8,16},{16,24},{24,32},{32,40},{40,48},{48,56},{56,64},{64,7... | collective-permute-start | bytes 3538952 | tf_op jit(solution)/shard_map/while/body/eval_jaxpr/ppermute | solution.py:9
  542.4 165.1 %reduce-scatter.4.cloned.1.call-start = ((), (), s32[]{:S(2)}) async-start(), calls=%async_computation.3 | async-start | bytes 3538944 | tf_op jit(solution)/shard_map/reduce_scatter | solution.py:98
  547.5 232.3 %reduce-scatter.8.cloned.1.call-start = ((), (), s32[]{:S(2)}) async-start(), calls=%async_computation.5 | async-start | bytes 6684672 | tf_op jit(solution)/shard_map/reduce_scatter | solution.py:90
  (76 other events, 503.3 us)
Sparse Core Ops, SparseCore 0:
  542.6 81.1 reduce-scatter.5
  628.2 79.2 reduce-scatter.3
  710.6 69.1 reduce-scatter.7
where the time goes:
time: 790 us; the launch traced here: 786 us
  waiting for transfers between devices  462 us (58%)
  matrix products  162 us (21%)
  local copies, waits for them, and re-layouts  99.8 us (13%)
  blocking collectives  24.6 us (3%)
  other arithmetic  21.1 us (3%)
  between operations  15.3 us (2%)
    ppermute x15, waiting for transfers between devices, shifted(): lax.ppermute(value, axis, [(i, (i + by) % count) for i in range(count)])  259 us
    while x165, local copies, waits for them, and re-layouts  84 us
    reduce_scatter x1, waiting for transfers between devices, shards(): lax.psum_scatter(input_total.astype(jnp.bfloat16), 'seq', scatter_dimensi...  81.7 us
    reduce_scatter x1, waiting for transfers between devices, shards(): lax.psum_scatter(down_buffer, 'blk', scatter_dimension=0, tiled=True)  72.3 us
    reduce_scatter x1, waiting for transfers between devices, shards(): lax.psum_scatter(in_buffer, 'blk', scatter_dimension=0, tiled=True)  49.1 us
    dot_general x32, matrix products, contract_rows(): lax.dot_general(left, right, (((0,), (0,)), ((), ())), preferred_element_...  46.4 us
    dot_general x16, matrix products, contract_cols(): lax.dot_general(left, right, (((1,), (1,)), ((), ())), preferred_element_...  43.1 us
    dot_general x16, matrix products, local_terms(): jnp.dot(inputs_rows, packed[:, :2 * unit_count], preferred_element_type=j...  37.1 us
  transfers between devices with their start and end apart: 18, of which 18 were waited for; matrix products, arithmetic and copies ran while one was open for 3% of the time, Pallas kernels for 0%

commit v1 on v0

v1 whole, which is shorter than its diff:
```python
import functools

import jax
import jax.numpy as jnp
from jax import lax
from jax.experimental import pallas as pl
from jax.experimental.pallas import tpu as pltpu
from jax.sharding import PartitionSpec as P

MESH = pl.DeviceIdType.MESH
BF16 = jnp.bfloat16
F32 = jnp.float32
NT = (((1,), (1,)), ((), ()))
NN = (((1,), (0,)), ((), ()))

L0, Z0 = (0, 0), (0, 1)
L2, Z2 = (3, 0), (3, 1)
CHUNKS = (0, 1, 2)
ALONG_X = (0, 2)


def l_at(step):
    return (1, (1 - step) // 2)


def z_at(step):
    return (2, (1 - step) // 2)


def kernel(
    x_hbm, g_hbm, wc_hbm, gate_hbm, up_hbm, down_hbm,
    gu_out, down_out, in_out, prob_out,
    X, G, WC, W, GB, AT, PT, DG, RZ, RZX, RX2, RXF, IG, SIB, YR2, YF, ZF, LH,
    PB, SIBP, PR2, PF, PZ,
    local_sem, send_sem, recv_sem,
    *, units, rows, feats, blocks,
):
    U = units
    rb, nb_dw, nb_ig = blocks
    part = rows // 8
    blk, seq = lax.axis_index("blk"), lax.axis_index("seq")
    c = lax.rem(blk, 2)
    x = lax.rem(blk // 2, 4)
    y = lax.rem(seq, 4)
    zh = seq // 4
    z = zh * 2 + blk // 8
    up = 1 - 2 * c

    def device(xx, yy, zz, cc):
        xx, yy, zz = lax.rem(xx + 8, 4), lax.rem(yy + 8, 4), lax.rem(zz + 8, 4)
        return ((lax.rem(zz, 2) * 4 + xx) * 2 + cc, (zz // 2) * 4 + yy)

    def along_x(step):
        return device(x + step, y, z, c)

    def along_y(step):
        return device(x, y + step, z, c)

    z_next, z_back, z_far = device(x, y, z + up, c), device(x, y, z - up, c), device(x, y, z + 2, c)
    sibling = device(x, y, z, 1 - c)
    turn = (1, up, -1)

    def chunk(ref, slot, j):
        pair, half = slot
        start = j * 2 * U + half * U
        if not isinstance(start, int):
            start = pl.multiple_of(start, U)
        return ref.at[pair, pl.ds(start, U), :]

    pending = []
    used = [0]

    def ids(count):
        used[0] += count
        return used[0] - count

    def transfer(src, dst, number, target):
        return pltpu.make_async_remote_copy(
            src_ref=src, dst_ref=dst, send_sem=send_sem.at[number], recv_sem=recv_sem.at[number],
            device_id=target, device_id_type=MESH,
        )

    def start(copy):
        copy.start()
        pending.append(copy)
        return copy

    n_l = ids(6)
    n_z0 = ids(3)
    n_l2 = ids(3)
    n_z = ids(6)
    n_z2 = ids(3)
    n_rz = ids(12)
    n_rzx = ids(3)
    n_rx2 = ids(3)
    n_rxf = ids(6)
    n_row = ids(3)
    n_sib = ids(2)
    n_sibp = ids(1)
    n_y2 = ids(4)
    n_yf = ids(4)
    n_yfp = ids(4)
    n_zf = ids(2)

    def side(step):
        return (1 - step) // 2

    own = (gate_hbm, up_hbm, down_hbm)

    def send_l(step, j):
        return transfer(own[j], chunk(W, l_at(-step), j), n_l + side(-step) * 3 + j, along_x(step))

    def send_z0(j):
        return transfer(own[j], chunk(W, Z0, j), n_z0 + j, z_next)

    def send_l2(j):
        return transfer(chunk(W, l_at(-turn[j]), j), chunk(W, L2, j), n_l2 + j, along_x(turn[j]))

    def send_z(step, j):
        return transfer(chunk(W, l_at(step), j), chunk(W, z_at(step), j), n_z + side(step) * 3 + j, z_next)

    def send_z2(j):
        if j in ALONG_X:
            return transfer(chunk(W, z_at(-turn[j]), j), chunk(W, Z2, j), n_z2 + j, along_x(turn[j]))
        return transfer(chunk(W, L2, j), chunk(W, Z2, j), n_z2 + j, z_next)

    def back_z(slot, which, j):
        return transfer(chunk(DG, slot, j), RZ.at[which, j], n_rz + which * 3 + j, z_back)

    def back_z2(j):
        return transfer(chunk(DG, Z2, j), RZX.at[j // 2], n_rzx + j, along_x(turn[j]))

    def back_l2(j):
        return transfer(chunk(DG, L2, j), RX2.at[j], n_rx2 + j, along_x(turn[j]))

    def back_l(step, j):
        return transfer(
            chunk(DG, l_at(step), j), RXF.at[side(step), j], n_rxf + side(step) * 3 + j, along_x(step)
        )

    def add_to(slot, j, *terms):
        ref = chunk(DG, slot, j)
        total = ref[...].astype(F32)
        for term in terms:
            total += term[...].astype(F32)
        ref[...] = total.astype(BF16)

    def forward(p, order):
        for first in order:
            here = pl.ds(pl.multiple_of(first, rb), rb)
            pre = lax.dot_general(X[here, :], W[p, 0 : 4 * U, :], NT, preferred_element_type=F32)
            back = lax.dot_general(G[here, :], W[p, 4 * U : 6 * U, :], NT, preferred_element_type=F32)
            gate_pre, up_pre = pre[:, : 2 * U], pre[:, 2 * U :]
            s = jax.nn.sigmoid(gate_pre)
            activated = gate_pre * s
            hidden = activated * up_pre
            product = hidden.astype(BF16).astype(F32) * back
            if p == 0:
                PT[here, :] = product
            else:
                PT[here, :] += product
            weight = WC[here, :]
            weighted = weight * back
            gate_back = weighted * up_pre * s * (1.0 + gate_pre * (1.0 - s))
            up_back = weighted * activated
            GB[p, here, 0 : 2 * U] = gate_back.astype(BF16)
            GB[p, here, 2 * U :] = up_back.astype(BF16)
            AT[:, here] = jnp.concatenate([gate_back, up_back, weight * hidden], axis=1).T.astype(BF16)

    def weight_terms(p):
        def body(i, carry):
            cols = pl.ds(pl.multiple_of(i * nb_dw, nb_dw), nb_dw)
            DG[p, 0 : 4 * U, cols] = lax.dot_general(
                AT[0 : 4 * U, :], X[:, cols], NN, preferred_element_type=F32
            ).astype(BF16)
            DG[p, 4 * U :, cols] = lax.dot_general(
                AT[4 * U :, :], G[:, cols], NN, preferred_element_type=F32
            ).astype(BF16)
            return carry

        lax.fori_loop(0, feats // nb_dw, body, 0)

    steps_y = (2, 1, -1, 0)

    def row_start(group, k, h):
        return pl.multiple_of(group * rows + (h * 4 + lax.rem(y + steps_y[k] + 4, 4)) * part, part)

    def row_terms(which, group, k0):
        for i in range(4):
            here = pl.ds(row_start(group, k0 + i // 2, i % 2), part)
            for p in range(4):
                LH[i * part : (i + 1) * part, p * 4 * U : (p + 1) * 4 * U] = GB[p, here, :]

        def body(n, carry):
            cols = pl.ds(pl.multiple_of(n * nb_ig, nb_ig), nb_ig)
            total = lax.dot_general(LH[:, 0 : 4 * U], W[0, 0 : 4 * U, cols], NN, preferred_element_type=F32)
            for p in range(1, 4):
                total += lax.dot_general(
                    LH[:, p * 4 * U : (p + 1) * 4 * U], W[p, 0 : 4 * U, cols], NN, preferred_element_type=F32
                )
            for i in range(4):
                IG[which, k0 + i // 2, i % 2, :, cols] = total[i * part : (i + 1) * part].astype(BF16)
            return carry

        lax.fori_loop(0, feats // nb_ig, body, 0)

    def prob_terms():
        ones = jnp.ones((8, 2 * U), F32)
        for which in range(2):
            group = c if which == 0 else 1 - c
            for k in range(4):
                for h in range(2):
                    here = pl.ds(row_start(group, k, h), part)
                    PB[which, k, h, :, 0:part] = lax.dot_general(
                        ones, PT[here, :], NT, preferred_element_type=F32, precision=lax.Precision.HIGHEST
                    )

    mine = pl.ds(pl.multiple_of(c * rows, rows), rows)
    locals_ = [
        pltpu.make_async_copy(own[j], chunk(W, L0, j), local_sem.at[j]) for j in CHUNKS
    ] + [
        pltpu.make_async_copy(x_hbm, X.at[mine, :], local_sem.at[3]),
        pltpu.make_async_copy(g_hbm, G.at[mine, :], local_sem.at[4]),
        pltpu.make_async_copy(wc_hbm, WC.at[mine, :], local_sem.at[5]),
    ]

    barrier = pltpu.get_barrier_semaphore()
    friends = (
        along_x(1), along_x(-1), along_y(1), along_y(-1), z_next, z_back, z_far, sibling,
    )
    for friend in friends:
        pl.semaphore_signal(barrier, inc=1, device_id=friend, device_id_type=MESH)
    for copy in locals_:
        copy.start()
    PB[...] = jnp.zeros_like(PB)
    pl.semaphore_wait(barrier, len(friends))

    for j in CHUNKS:
        for step in (1, -1):
            start(send_l(step, j))
        start(send_z0(j))
    row_copies = [
        start(transfer(x_hbm, X.at[mine, :], n_row, sibling)),
        start(transfer(g_hbm, G.at[mine, :], n_row + 1, sibling)),
        start(transfer(wc_hbm, WC.at[mine, :], n_row + 2, sibling)),
    ]

    def pass_l(j):
        for step in (1, -1):
            send_l(-step, j).wait_recv()
            start(send_z(step, j))
        start(send_l2(j))

    def pass_z(j):
        for step in (1, -1):
            send_z(step, j).wait_recv()
        if j in ALONG_X:
            start(send_z2(j))

    def pass_l2(j):
        send_l2(j).wait_recv()
        if j not in ALONG_X:
            start(send_z2(j))

    own_first, other_first = c * rows, (1 - c) * rows
    pass_l(0)
    for copy in locals_:
        copy.wait()
    for j in CHUNKS:
        send_z0(j).wait_recv()
    forward(0, [own_first])
    pass_l(1)
    for copy in row_copies:
        copy.wait_recv()
    forward(0, [other_first])
    weight_terms(0)
    pass_l(2)
    pass_z(0)
    forward(1, [0, rows])
    pass_l2(0)
    pass_z(1)
    pass_l2(1)
    weight_terms(1)
    pass_l2(2)
    pass_z(2)
    forward(2, [0, rows])
    weight_terms(2)
    for j in ALONG_X:
        start(back_z(z_at(-turn[j]), 1 + side(-turn[j]), j))
    for step in (1, -1):
        start(back_z(z_at(step), 1 + side(step), 1))
    for j in CHUNKS:
        send_z2(j).wait_recv()
    forward(3, [0, rows])
    weight_terms(3)
    for j in ALONG_X:
        start(back_z2(j))
        start(back_l2(j))
    start(back_z(Z2, 3, 1))

    sib_copies = []
    row_terms(1, 1 - c, 0)
    sib_copies.append(start(transfer(IG.at[1, 0:2], SIB.at[0:2], n_sib, sibling)))
    prob_terms()
    sib_p = start(transfer(PB.at[1], SIBP, n_sibp, sibling))
    row_terms(1, 1 - c, 2)
    sib_copies.append(start(transfer(IG.at[1, 2:4], SIB.at[2:4], n_sib + 1, sibling)))
    for j in ALONG_X:
        back_z2(j).wait_recv()
        add_to(z_at(turn[j]), j, RZX.at[j // 2])
        start(back_z(z_at(turn[j]), 1 + side(turn[j]), j))
    for j in CHUNKS:
        start(back_z(Z0, 0, j))
    row_terms(0, c, 0)
    for j in ALONG_X:
        back_z(z_at(-turn[j]), 1 + side(-turn[j]), j).wait_recv()
        add_to(l_at(-turn[j]), j, RZ.at[1 + side(-turn[j]), j])
        start(back_l(-turn[j], j))
    row_terms(0, c, 2)

    def add_sib(k):
        IG[0, k] = (IG[0, k].astype(F32) + SIB[k].astype(F32)).astype(BF16)

    def add_row(k, h, ref):
        IG[0, k, h] = (IG[0, k, h].astype(F32) + ref[...].astype(F32)).astype(BF16)

    def y_far(h):
        step = 1 - 2 * h
        return (
            transfer(IG.at[0, 0, h], YR2.at[h], n_y2 + h, along_y(step)),
            transfer(PB.at[0, 0, h], PR2.at[h], n_y2 + 2 + h, along_y(step)),
        )

    def y_last(k, h):
        step = steps_y[k]
        return (
            transfer(IG.at[0, k, h], YF.at[k - 1, h], n_yf + (k - 1) * 2 + h, along_y(step)),
            transfer(PB.at[0, k, h], PF.at[k - 1, h], n_yfp + (k - 1) * 2 + h, along_y(step)),
        )

    sib_copies[0].wait_recv()
    sib_p.wait_recv()
    PB[0] = PB[0] + SIBP[...]
    add_sib(0)
    for h in range(2):
        for copy in y_far(h):
            start(copy)
    add_sib(1)
    for copy in y_last(1, 1):
        start(copy)
    sib_copies[1].wait_recv()
    add_sib(2)
    for copy in y_last(2, 0):
        start(copy)
    add_sib(3)

    for step in (1, -1):
        back_z(z_at(step), 1 + side(step), 1).wait_recv()
        add_to(l_at(step), 1, RZ.at[1 + side(step), 1])
    start(back_l(-turn[1], 1))
    back_z(Z2, 3, 1).wait_recv()
    add_to(L2, 1, RZ.at[3, 1])
    start(back_l2(1))
    for j in ALONG_X:
        back_z(z_at(turn[j]), 1 + side(turn[j]), j).wait_recv()
        back_l2(j).wait_recv()
        add_to(l_at(turn[j]), j, RZ.at[1 + side(turn[j]), j], RX2.at[j])
        start(back_l(turn[j], j))
    for k, h in ((1, 0), (2, 1)):
        for copy in y_far(h):
            copy.wait_recv()
        add_row(k, h, YR2.at[h])
        PB[0, k, h] = PB[0, k, h] + PR2[h]
        for copy in y_last(k, h):
            start(copy)
    back_l2(1).wait_recv()
    add_to(l_at(turn[1]), 1, RX2.at[1])
    start(back_l(turn[1], 1))
    for k in (1, 2):
        for h in range(2):
            for copy in y_last(k, h):
                copy.wait_recv()
    IG[0, 3] = (IG[0, 3].astype(F32) + YF[0].astype(F32) + YF[1].astype(F32)).astype(BF16)
    PB[0, 3] = PB[0, 3] + PF[0] + PF[1]
    z_copies = (
        start(transfer(IG.at[0, 3, 1 - zh], ZF, n_zf, z_far)),
        start(transfer(PB.at[0, 3, 1 - zh], PZ, n_zf + 1, z_far)),
    )
    for j in CHUNKS:
        back_z(Z0, 0, j).wait_recv()
        for step in (1, -1):
            back_l(step, j).wait_recv()
        total = chunk(DG, L0, j)[...].astype(F32) + RZ[0, j].astype(F32)
        total += RXF[0, j].astype(F32) + RXF[1, j].astype(F32)
        if j < 2:
            gu_out[j * U : (j + 1) * U, :] = total.astype(BF16)
        else:
            down_out[...] = total.astype(BF16)
    for copy in z_copies:
        copy.wait_recv()
    in_out[...] = (IG[0, 3, zh].astype(F32) + ZF[...].astype(F32)).astype(BF16)
    prob_out[...] = PB[0, 3, zh] + PZ[...]
    for copy in pending:
        copy.wait_send()


N_SEMS = 65


def exchange(row_inputs, row_grads, weight_cols, gate_t, up_t, down, blocks):
    rows, feats = row_inputs.shape
    units = down.shape[0]
    part = rows // 8
    any_space = pl.BlockSpec(memory_space=pl.ANY)
    vmem = pl.BlockSpec(memory_space=pltpu.VMEM)
    piece = (units, feats)
    slab = (part, feats)
    tile = (8, 128)

    def held(*shape, kind=BF16):
        return pltpu.VMEM(shape, kind)

    return pl.pallas_call(
        functools.partial(kernel, units=units, rows=rows, feats=feats, blocks=blocks),
        out_shape=(
            jax.ShapeDtypeStruct((2 * units, feats), BF16),
            jax.ShapeDtypeStruct(piece, BF16),
            jax.ShapeDtypeStruct(slab, BF16),
            jax.ShapeDtypeStruct(tile, F32),
        ),
        in_specs=[any_space] * 6,
        out_specs=(vmem,) * 4,
        scratch_shapes=[
            held(2 * rows, feats),
            held(2 * rows, feats),
            held(2 * rows, 128, kind=F32),
            held(4, 6 * units, feats),
            held(4, 2 * rows, 4 * units),
            held(6 * units, 2 * rows),
            held(2 * rows, 2 * units, kind=F32),
            held(4, 6 * units, feats),
            held(4, 3, *piece),
            held(2, *piece),
            held(3, *piece),
            held(2, 3, *piece),
            held(2, 4, 2, *slab),
            held(4, 2, *slab),
            held(2, *slab),
            held(2, 2, *slab),
            held(*slab),
            held(4 * part, 16 * units),
            held(2, 4, 2, *tile, kind=F32),
            held(4, 2, *tile, kind=F32),
            held(2, *tile, kind=F32),
            held(2, 2, *tile, kind=F32),
            held(*tile, kind=F32),
            pltpu.SemaphoreType.DMA((6,)),
            pltpu.SemaphoreType.DMA((N_SEMS,)),
            pltpu.SemaphoreType.DMA((N_SEMS,)),
        ],
        compiler_params=pltpu.CompilerParams(
            collective_id=0, has_side_effects=True, vmem_limit_bytes=63 << 20
        ),
        cost_estimate=pl.CostEstimate(
            flops=16 * 2 * rows * 8 * units * feats, bytes_accessed=24 * rows * feats, transcendentals=16 * rows * units
        ),
        name="exchange",
    )(row_inputs, row_grads, weight_cols, gate_t, up_t, down)


def shards(blocks, row_inputs, row_grads, gate_prob, live_counts, gate_weight, up_weight, down_weight):
    rows = row_inputs.shape[0]
    units = down_weight.shape[0]
    part = rows // 8
    live = jnp.arange(rows, dtype=jnp.int32) < live_counts[0]
    weight_rows = jnp.where(live, gate_prob, 0.0)
    weight_cols = jnp.broadcast_to(weight_rows[:, None], (rows, 128))
    gu, down_grad, input_grad, prob = exchange(
        row_inputs, row_grads, weight_cols, gate_weight.T, up_weight.T, down_weight, blocks
    )
    first = lax.axis_index("seq") * part
    here = first + jnp.arange(part, dtype=jnp.int32)
    prob_grad = jnp.where(here < live_counts[0], prob[0, :part], 0.0)
    return (input_grad, prob_grad, gu[:units].T, gu[units:].T, down_grad)


def solution(mesh, blocks=(512, 1024, 1024)):
    return jax.shard_map(
        functools.partial(shards, blocks),
        mesh=mesh,
        in_specs=(
            P("blk", None),
            P("blk", None),
            P("blk"),
            P("blk"),
            P(None, ("blk", "seq")),
            P(None, ("blk", "seq")),
            P(("blk", "seq"), None),
        ),
        out_specs=(
            P(("blk", "seq"), None),
            P(("blk", "seq")),
            P(None, ("blk", "seq")),
            P(None, ("blk", "seq")),
            P(("blk", "seq"), None),
        ),
        check_vma=False,
    )
```

time: 790 us -> 126 us (0.16)
  waiting for transfers between devices: 462 us -> 0 us
  matrix products: 162 us -> 0 us
  Pallas kernels: 0 us -> 116 us
  local copies, waits for them, and re-layouts: 99.8 us -> 6.41 us
  blocking collectives: 24.6 us -> 0 us
  other arithmetic: 21.1 us -> 1.88 us
  between operations: 15.3 us -> 1.29 us
    ppermute x15 -> x0, waiting for transfers between devices: 259 us -> none  [shifted(): lax.ppermute(value, axis, [(i, (i + by) % count) for i in range(count)])]
    reduce_scatter x3 -> x0, waiting for transfers between devices: 203 us -> none  [the longest x1 81.7 us: shards(): lax.psum_scatter(input_total.astype(jnp.bfloat16), 'seq', scatter_dimensi...]
    dot_general x80 -> x0, matrix products: 162 us -> none  [the longest x32 46.4 us: contract_rows(): lax.dot_general(left, right, (((0,), (0,)), ((), ())), preferred_element_...]
    pallas_call x0 -> x1, Pallas kernels: none -> 116 us  [exchange(): pl.pallas_call(functools.partial(kernel, units=units, rows=rows, feats=fe...]
    while x165 -> x0, local copies, waits for them, and re-layouts: 84 us -> none
    unnamed x1 -> x0, blocking collectives: 24.6 us -> none
    convert_element_type x20 -> x0, other arithmetic: 18.5 us -> none  [the longest x16 12 us: shards(): (jnp.arange(row_count, dtype=jnp.int32) < live_count).astype(jnp.float32)]
  transfers between devices with their start and end apart: 18 -> 0, of which waited for: 18 -> 0; matrix products, arithmetic and copies ran while one was open for 3% -> 0% of each run, Pallas kernels for 0% -> 0%
where the time goes in v1:
time: 126 us; the launch traced here: 125 us
  Pallas kernels  116 us (92%)
  local copies, waits for them, and re-layouts  6.41 us (5%)
  other arithmetic  1.88 us (1%)
  between operations  1.29 us (1%)
    pallas_call x1, Pallas kernels, exchange(): pl.pallas_call(functools.partial(kernel, units=units, rows=rows, feats=fe...  116 us
    unnamed x2, local copies, waits for them, and re-layouts  3.53 us

profile of v1, /device:TPU:32, one launch (start us, length us, event | category | flops | bytes accessed | tf_op | source)
XLA Modules:
  0.0 125.4 jit_solution(532233472974420486)
XLA Ops:
  1.3 0.7 fusion
  2.0 0.8 broadcast_in_dim.15.wc_hbm
  2.8 115.9 %exchange.1 = (bf16[128,3072]{1,0:T(8,128)(2,1)}, bf16[64,3072]{1,0:T(8,128)(2,1)}, bf16[64,3072]{1,0:T(8,128)(2,1)}, f32[8,128]{1,0:T(8,128)}) custom-call(bf16[512,3072]{1,0:T(8,128)(2,1)} %x_hbm.1, bf16[512,3072]{1,0:T(8,128)(2,1)} %g_hbm.1, f32[512,128]{1,0:T(8,128)} %broadcast_in_dim.15.wc_hbm, bf16[64,3072]{1,0:T(8,128)(2,1)} %bitcast.11, ...), custom_call_target="tpu_custom_call" | custom-call | flops 25769803776 | bytes 37748736 | tf_op jit(solution)/shard_map/exchange/pallas_call | solution.py:423
  118.7 1.2 compare_select_fusion
  119.9 2.0 %slice_bitcast_fusion = (bf16[3072,64]{0,1:T(8,128)(2,1)}, bf16[3072,64]{0,1:T(8,128)(2,1)}) fusion(bf16[128,3072]{1,0:T(8,128)(2,1)} %get-tuple-element.11), kind=kLoop, calls=%fused_computation | loop fusion | bytes 1572864 | tf_op jit(solution)/shard_map/transpose | solution.py:484
  121.9 1.8 %copy.15 = bf16[64,3072]{1,0:T(8,128)(2,1)} copy(bf16[64,3072]{1,0:T(8,128)(2,1)} %get-tuple-element.20) | data formatting | bytes 786432
  123.7 1.8 %copy.16 = bf16[64,3072]{1,0:T(8,128)(2,1)} copy(bf16[64,3072]{1,0:T(8,128)(2,1)} %get-tuple-element.24) | data formatting | bytes 786432

commit v2 on v0

v2 whole, which is shorter than its diff:
```python
import functools

import jax
import jax.numpy as jnp
from jax import lax
from jax.experimental import pallas as pl
from jax.experimental.pallas import tpu as pltpu
from jax.sharding import PartitionSpec as P

MESH = pl.DeviceIdType.MESH
BF16 = jnp.bfloat16
F32 = jnp.float32
NT = (((1,), (1,)), ((), ()))
NN = (((1,), (0,)), ((), ()))

(
    GO_L, GO_Z0, GO_Z, GO_L2, GO_Z2, BACK_Z0, BACK_Z, BACK_Z2, BACK_X2, BACK_L2, BACK_L,
    ROWS_X, ROWS_G, ROWS_W, TWIN, ALONG_Y, FAR_Z, PROB,
) = range(18)

L0, Z0 = (0, 0), (0, 1)
L2, Z2 = (3, 0), (3, 1)
CHUNKS = range(6)
TURN = (1, 1, 1, -1, -1, -1)
ALONG_X = (0, 1, 4, 5)
ORDER = (
    63, 61, 45, 48, 15, 46, 60, 1, 90, 64, 3, 62, 76, 18, 31, 47, 49, 33, 16, 2, 4, 19, 77, 65, 78, 6, 50, 80, 34,
    21, 35, 32, 81, 5, 66, 79, 17, 95, 96, 98, 0, 75, 30, 20, 97, 100, 99, 51, 101, 23, 102, 53, 36, 91, 55, 92, 68,
    93, 94, 52, 54, 24, 104, 103, 69, 106, 71, 115, 38, 70, 105, 26, 107, 67, 108, 25, 116, 41, 118, 56, 8, 109, 86,
    85, 111, 112, 117, 132, 124, 40, 42, 10, 110, 131, 125, 119, 27, 113, 22, 72, 120, 82, 57, 122, 133, 114, 83, 9,
    11, 28, 121, 134, 58, 127, 128, 37, 136, 12, 43, 123, 129, 135, 73, 84, 39, 87, 13, 7, 126, 29, 137, 59, 88,
    130, 74, 44, 14, 89, 138,
)


def l_at(step):
    return (1, (1 - step) // 2)


def z_at(step):
    return (2, (1 - step) // 2)


def kernel(
    x_hbm, g_hbm, prob_hbm, count_hbm, gate_hbm, up_hbm, down_hbm,
    gate_out, up_out, down_out, in_out, prob_out,
    X, G, WC, W, GB, AT, PT, DG, RZ, RZX, RX2, RXF, IG, SIB, YR2, YF, ZF, LH,
    PB, SIBP, PR2, PF, PZ, PV, count_ref,
    local_sem, send_sem, recv_sem,
    *, units, rows, feats, blocks,
):
    U = units
    nb_dw, nb_ig = blocks
    part = rows // 8
    blk, seq = lax.axis_index("blk"), lax.axis_index("seq")
    c = lax.rem(blk, 2)
    x = lax.rem(blk // 2, 4)
    y = lax.rem(seq, 4)
    zh = seq // 4
    z = zh * 2 + blk // 8
    up = 1 - 2 * c

    def device(xx, yy, zz, cc):
        xx, yy, zz = lax.rem(xx + 8, 4), lax.rem(yy + 8, 4), lax.rem(zz + 8, 4)
        return ((lax.rem(zz, 2) * 4 + xx) * 2 + cc, (zz // 2) * 4 + yy)

    def along_x(step):
        return device(x + step, y, z, c)

    def along_y(step):
        return device(x, y + step, z, c)

    z_next, z_back, z_far = device(x, y, z + up, c), device(x, y, z - up, c), device(x, y, z + 2, c)
    sibling = device(x, y, z, 1 - c)
    half = U // 2

    def chunk(ref, slot, h):
        pair, place = slot
        return ref.at[pair, pl.ds(h // 2 * 2 * U + place * U + h % 2 * half, half), :]

    def side(step):
        return (1 - step) // 2

    routes = {}
    pending = []
    here = set()

    def route(name, src, dst, target):
        number = len(routes)
        routes[name] = lambda: pltpu.make_async_remote_copy(
            src_ref=src, dst_ref=dst, send_sem=send_sem.at[number], recv_sem=recv_sem.at[number],
            device_id=target, device_id_type=MESH,
        )

    def send(*names):
        for name in names:
            copy = routes[name]()
            copy.start()
            pending.append(copy)

    def need(*names):
        for name in names:
            if name not in here:
                here.add(name)
                routes[name]().wait_recv()

    for h in CHUNKS:
        t = TURN[h]
        own = (gate_hbm, up_hbm, down_hbm)[h // 2].at[pl.ds(h % 2 * half, half), :]
        route((GO_Z0, h), own, chunk(W, Z0, h), z_next)
        route((BACK_Z0, h), chunk(DG, Z0, h), RZ.at[0, h], z_back)
        for e in (1, -1):
            route((GO_L, e, h), own, chunk(W, l_at(e), h), along_x(-e))
            route((GO_Z, e, h), chunk(W, l_at(e), h), chunk(W, z_at(e), h), z_next)
            route((BACK_Z, e, h), chunk(DG, z_at(e), h), RZ.at[1 + side(e), h], z_back)
            route((BACK_L, e, h), chunk(DG, l_at(e), h), RXF.at[side(e), h], along_x(e))
        route((GO_L2, h), chunk(W, l_at(-t), h), chunk(W, L2, h), along_x(t))
        route((BACK_L2, h), chunk(DG, L2, h), RX2.at[h], along_x(t))
        if h in ALONG_X:
            route((GO_Z2, h), chunk(W, z_at(-t), h), chunk(W, Z2, h), along_x(t))
            route((BACK_X2, h), chunk(DG, Z2, h), RZX.at[ALONG_X.index(h)], along_x(t))
        else:
            route((GO_Z2, h), chunk(W, L2, h), chunk(W, Z2, h), z_next)
            route((BACK_Z2, h), chunk(DG, Z2, h), RZ.at[3, h], z_back)

    mine = pl.ds(pl.multiple_of(c * rows, rows), rows)
    route(ROWS_X, x_hbm, X.at[mine, :], sibling)
    route(ROWS_G, g_hbm, G.at[mine, :], sibling)
    route(ROWS_W, WC.at[mine, :], WC.at[mine, :], sibling)
    for k in range(4):
        route((TWIN, k), IG.at[1, k], SIB.at[k], sibling)
    route((TWIN, PROB), PB.at[1], SIBP, sibling)

    def halves(ref):
        return [ref.at[pl.ds(q * (part // 2), part // 2), :] for q in range(2)]

    for k, h in ((0, 0), (0, 1), (1, 0), (1, 1), (2, 0), (2, 1)):
        step = (1 if h == 0 else -1) if k == 0 else (1 if k == 1 else -1)
        dst, dst_p = (YR2.at[h], PR2.at[h]) if k == 0 else (YF.at[k - 1, h], PF.at[k - 1, h])
        for q, (a, b) in enumerate(zip(halves(IG.at[0, k, h]), halves(dst))):
            route((ALONG_Y, k, h, q), a, b, along_y(step))
        route((ALONG_Y, k, h, PROB), PB.at[0, k, h], dst_p, along_y(step))
    for q, (a, b) in enumerate(zip(halves(IG.at[0, 3, 1 - zh]), halves(ZF))):
        route((FAR_Z, q), a, b, z_far)
    route((FAR_Z, PROB), PB.at[0, 3, 1 - zh], PZ, z_far)
    assert len(routes) == send_sem.shape[0]

    def add_into(out, ref, *terms):
        total = ref[...].astype(F32)
        for term in terms:
            total += term[...].astype(F32)
        out[...] = total.astype(BF16)

    def add_to(ref, *terms):
        add_into(ref, ref, *terms)

    counted = set()

    def forward(p, which, first):
        lines = pl.ds(pl.multiple_of(first, rows), rows)
        pre = lax.dot_general(X[lines, :], W[p, 0 : 4 * U, :], NT, preferred_element_type=F32)
        back = lax.dot_general(G[lines, :], W[p, 4 * U : 6 * U, :], NT, preferred_element_type=F32)
        gate_pre, up_pre = pre[:, : 2 * U], pre[:, 2 * U :]
        s = jax.nn.sigmoid(gate_pre)
        activated = gate_pre * s
        hidden = activated * up_pre
        product = hidden.astype(BF16).astype(F32) * back
        if which in counted:
            PT[lines, :] += product
        else:
            PT[lines, :] = product
        counted.add(which)
        weight = WC[lines, :]
        weighted = weight * back
        gate_back = weighted * up_pre * s * (1.0 + gate_pre * (1.0 - s))
        up_back = weighted * activated
        GB[p, lines, 0 : 2 * U] = gate_back.astype(BF16)
        GB[p, lines, 2 * U :] = up_back.astype(BF16)
        AT[:, lines] = jnp.concatenate([gate_back, up_back, weight * hidden], axis=1).T.astype(BF16)

    def weight_terms(p, first, last, rows_ref):
        def body(i, carry):
            cols = pl.ds(pl.multiple_of(i * nb_dw, nb_dw), nb_dw)
            DG[p, first:last, cols] = lax.dot_general(
                AT[first:last, :], rows_ref[:, cols], NN, preferred_element_type=F32
            ).astype(BF16)
            return carry

        lax.fori_loop(0, feats // nb_dw, body, 0)

    steps_y = (2, 1, -1, 0)

    def row_start(group, k, h):
        return pl.multiple_of(group * rows + (h * 4 + lax.rem(y + steps_y[k] + 4, 4)) * part, part)

    def row_terms(which, group, k0, pairs):
        for i in range(4):
            here = pl.ds(row_start(group, k0 + i // 2, i % 2), part)
            for n, p in enumerate(pairs):
                LH[i * part : (i + 1) * part, n * 4 * U : (n + 1) * 4 * U] = GB[p, here, :]

        def body(n, carry):
            cols = pl.ds(pl.multiple_of(n * nb_ig, nb_ig), nb_ig)
            total = lax.dot_general(
                LH[:, 0 : 4 * U], W[pairs[0], 0 : 4 * U, cols], NN, preferred_element_type=F32
            ) + lax.dot_general(
                LH[:, 4 * U :], W[pairs[1], 0 : 4 * U, cols], NN, preferred_element_type=F32
            )
            for i in range(4):
                term = total[i * part : (i + 1) * part]
                if pairs[0]:
                    term += IG[which, k0 + i // 2, i % 2, :, cols].astype(F32)
                IG[which, k0 + i // 2, i % 2, :, cols] = term.astype(BF16)
            return carry

        lax.fori_loop(0, feats // nb_ig, body, 0)

    def prob_terms():
        ones = jnp.ones((8, 2 * U), F32)
        for which in range(2):
            group = c if which == 0 else 1 - c
            for k in range(4):
                for h in range(2):
                    here = pl.ds(row_start(group, k, h), part)
                    PB[which, k, h, :, 0:part] = lax.dot_general(
                        ones, PT[here, :], NT, preferred_element_type=F32, precision=lax.Precision.HIGHEST
                    )

    locals_ = [
        pltpu.make_async_copy(ref, W.at[0, pl.ds(j * 2 * U, U), :], local_sem.at[j])
        for j, ref in enumerate((gate_hbm, up_hbm, down_hbm))
    ] + [
        pltpu.make_async_copy(x_hbm, X.at[mine, :], local_sem.at[3]),
        pltpu.make_async_copy(g_hbm, G.at[mine, :], local_sem.at[4]),
    ]
    gates = [
        pltpu.make_async_copy(prob_hbm, PV, local_sem.at[5]),
        pltpu.make_async_copy(count_hbm, count_ref, local_sem.at[6]),
    ]
    tasks = []

    def hand_on(needs, copy):
        @tasks.append
        def _():
            need(*needs)
            send(copy)

    def add_on(needs, ref, terms, copy):
        @tasks.append
        def _():
            need(*needs)
            add_to(ref, *terms)
            send(copy)

    both = (1, -1)
    arrivals = (
        [(GO_Z0, h) for h in CHUNKS],
        [(GO_L, e, h) for e in both for h in CHUNKS],
        [(GO_Z, e, h) for e in both for h in CHUNKS],
        [(k, h) for k in (GO_L2, GO_Z2) for h in CHUNKS],
    )
    for h in CHUNKS:
        t = TURN[h]
        hand_on((), (GO_Z0, h))
        for e in both:
            hand_on((), (GO_L, e, h))
            hand_on(((GO_L, e, h),), (GO_Z, e, h))
        hand_on(((GO_L, -t, h),), (GO_L2, h))
        hand_on(((GO_Z, -t, h) if h in ALONG_X else (GO_L2, h),), (GO_Z2, h))
        hand_on((), (BACK_Z0, h))
        hand_on((), (BACK_Z, -t, h))
        add_on(((BACK_Z, -t, h),), chunk(DG, l_at(-t), h), (RZ.at[1 + side(-t), h],), (BACK_L, -t, h)
        )
        if h in ALONG_X:
            hand_on((), (BACK_X2, h))
            hand_on((), (BACK_L2, h))
            add_on(((BACK_X2, h),), chunk(DG, z_at(t), h), (RZX.at[ALONG_X.index(h)],), (BACK_Z, t, h)
            )
        else:
            hand_on((), (BACK_Z, t, h))
            hand_on((), (BACK_Z2, h))
            add_on(((BACK_Z2, h),), chunk(DG, L2, h), (RZ.at[3, h],), (BACK_L2, h))
        add_on(((BACK_Z, t, h), (BACK_L2, h)), chunk(DG, l_at(t), h),
            (RZ.at[1 + side(t), h], RX2.at[h]), (BACK_L, t, h),
        )

        @tasks.append
        def _(h=h):
            need((BACK_Z0, h), (BACK_L, 1, h), (BACK_L, -1, h))
            out = (gate_out, up_out, down_out)[h // 2].at[pl.ds(h % 2 * half, half), :]
            add_into(out, chunk(DG, L0, h), RZ.at[0, h], RXF.at[0, h], RXF.at[1, h])

    @tasks.append
    def _():
        send(ROWS_X, ROWS_G)
        for copy in gates:
            copy.wait()
        for q in range(rows // 128):
            lines = pl.ds(pl.multiple_of(c * rows + q * 128, 128), 128)
            weights = jnp.broadcast_to(PV[q : q + 1, :], (128, 128)).T
            live = lax.broadcasted_iota(jnp.int32, (128, 128), 0) + q * 128 < count_ref[0]
            WC[lines, :] = jnp.where(live, weights, 0.0)
        send(ROWS_W)
        for copy in locals_:
            copy.wait()

    for p in range(4):
        for which in range(2):

            @tasks.append
            def _(p=p, which=which):
                need(*arrivals[p], *((ROWS_X, ROWS_G, ROWS_W) if which else ()))
                forward(p, which, (1 - c) * rows if which else c * rows)

        @tasks.append
        def _(p=p):
            weight_terms(p, 0, 4 * U, X)

        @tasks.append
        def _(p=p):
            weight_terms(p, 4 * U, 6 * U, G)

    for index in (1, 0):
        for k in (0, 2):
            for pairs in ((0, 1), (2, 3)):

                @tasks.append
                def _(index=index, k=k, pairs=pairs):
                    row_terms(index, 1 - c if index else c, k, pairs)

    @tasks.append
    def _():
        prob_terms()

    for k in range(4):

        @tasks.append
        def _(k=k):
            if k == 0:
                send((TWIN, PROB))
            send((TWIN, k))

        @tasks.append
        def _(k=k):
            if k == 0:
                need((TWIN, PROB))
                PB[0] = PB[0] + SIBP[...]
            need((TWIN, k))
            add_to(IG.at[0, k], SIB.at[k])

    for q in range(2):
        for k, h in ((0, 0), (0, 1), (1, 1), (2, 0)):

            @tasks.append
            def _(k=k, h=h, q=q):
                if q == 0:
                    send((ALONG_Y, k, h, PROB))
                send((ALONG_Y, k, h, q))

        for k, h in ((1, 0), (2, 1)):

            @tasks.append
            def _(k=k, h=h, q=q):
                if q == 0:
                    need((ALONG_Y, 0, h, PROB))
                    PB[0, k, h] = PB[0, k, h] + PR2[h]
                    send((ALONG_Y, k, h, PROB))
                need((ALONG_Y, 0, h, q))
                add_to(halves(IG.at[0, k, h])[q], halves(YR2.at[h])[q])
                send((ALONG_Y, k, h, q))

        @tasks.append
        def _(q=q):
            ends = ((1, 0), (1, 1), (2, 0), (2, 1))
            if q == 0:
                need(*((ALONG_Y, k, h, PROB) for k, h in ends))
                PB[0, 3] = PB[0, 3] + PF[0] + PF[1]
                send((FAR_Z, PROB))
            need(*((ALONG_Y, k, h, q) for k, h in ends))
            for h in range(2):
                add_to(halves(IG.at[0, 3, h])[q], halves(YF.at[0, h])[q], halves(YF.at[1, h])[q])
            send((FAR_Z, q))

    @tasks.append
    def _():
        need((FAR_Z, PROB), (FAR_Z, 0), (FAR_Z, 1))
        add_into(in_out, IG.at[0, 3, zh], ZF)
        lane = lax.broadcasted_iota(jnp.int32, (8, 128), 1)
        prob_out[...] = jnp.where(seq * part + lane < count_ref[0], PB[0, 3, zh] + PZ[...], 0.0)

    barrier = pltpu.get_barrier_semaphore()
    friends = (
        along_x(1), along_x(-1), along_y(1), along_y(-1), z_next, z_back, z_far, sibling,
    )
    for friend in friends:
        pl.semaphore_signal(barrier, inc=1, device_id=friend, device_id_type=MESH)
    for copy in gates + locals_:
        copy.start()
    PB[...] = jnp.zeros_like(PB)
    pl.semaphore_wait(barrier, len(friends))
    assert sorted(ORDER) == list(range(len(tasks)))
    for number in ORDER:
        tasks[number]()
    for copy in pending:
        copy.wait_send()


def finish(gate_in, up_in, down_in, rows_in, prob_in, gate_out, up_out, down_out, rows_out, prob_out, sems):
    pairs = ((gate_in, gate_out), (up_in, up_out), (down_in, down_out), (rows_in, rows_out))
    copies = [pltpu.make_async_copy(src, dst, sems.at[n]) for n, (src, dst) in enumerate(pairs)]
    for copy in copies:
        copy.start()
    prob_out[...] = prob_in[0, 0 : prob_out.shape[0]]
    for copy in copies:
        copy.wait()


N_SEMS = 113
VMEM_LIMIT = 61 << 20


def exchange(row_inputs, row_grads, gate_prob, live_counts, gate_t, up_t, down, blocks):
    rows, feats = row_inputs.shape
    units = down.shape[0]
    part = rows // 8
    any_space = pl.BlockSpec(memory_space=pl.ANY)
    piece = (units, feats)
    slab = (part, feats)
    tile = (8, 128)

    def held(*shape, kind=BF16):
        return pltpu.VMEM(shape, kind)

    return pl.pallas_call(
        functools.partial(kernel, units=units, rows=rows, feats=feats, blocks=blocks),
        out_shape=(
            held(*piece),
            held(*piece),
            held(*piece),
            held(*slab),
            held(*tile, kind=F32),
        ),
        in_specs=[any_space] * 7,
        out_specs=(pl.BlockSpec(memory_space=pltpu.VMEM),) * 5,
        scratch_shapes=[
            held(2 * rows, feats),
            held(2 * rows, feats),
            held(2 * rows, 128, kind=F32),
            held(4, 6 * units, feats),
            held(4, 2 * rows, 4 * units),
            held(6 * units, 2 * rows),
            held(2 * rows, 2 * units, kind=F32),
            held(4, 6 * units, feats),
            held(4, 6, units // 2, feats),
            held(len(ALONG_X), units // 2, feats),
            held(6, units // 2, feats),
            held(2, 6, units // 2, feats),
            held(2, 4, 2, *slab),
            held(4, 2, *slab),
            held(2, *slab),
            held(2, 2, *slab),
            held(*slab),
            held(4 * part, 8 * units),
            held(2, 4, 2, *tile, kind=F32),
            held(4, 2, *tile, kind=F32),
            held(2, *tile, kind=F32),
            held(2, 2, *tile, kind=F32),
            held(*tile, kind=F32),
            held(rows // 128, 128, kind=F32),
            pltpu.SMEM((1,), jnp.int32),
            pltpu.SemaphoreType.DMA((7,)),
            pltpu.SemaphoreType.DMA((N_SEMS,)),
            pltpu.SemaphoreType.DMA((N_SEMS,)),
        ],
        compiler_params=pltpu.CompilerParams(
            collective_id=0, has_side_effects=True, vmem_limit_bytes=VMEM_LIMIT
        ),
        cost_estimate=pl.CostEstimate(
            flops=16 * 2 * rows * 8 * units * feats, bytes_accessed=24 * rows * feats, transcendentals=16 * rows * units
        ),
        name="exchange",
    )(row_inputs, row_grads, gate_prob.reshape(-1, 128), live_counts, gate_t, up_t, down)


def hand_over(gate_t, up_t, down, rows_out, prob, part):
    any_space = pl.BlockSpec(memory_space=pl.ANY)
    vmem = pl.BlockSpec(memory_space=pltpu.VMEM)
    arrays = (gate_t, up_t, down, rows_out)
    return pl.pallas_call(
        finish,
        out_shape=tuple(jax.ShapeDtypeStruct(a.shape, a.dtype) for a in arrays)
        + (jax.ShapeDtypeStruct((part,), F32),),
        in_specs=[vmem] * 5,
        out_specs=(any_space,) * 4 + (vmem,),
        scratch_shapes=[pltpu.SemaphoreType.DMA((4,))],
        name="hand_over",
    )(*(pltpu.with_memory_space_constraint(a, pltpu.VMEM) for a in (*arrays, prob)))


def shards(blocks, row_inputs, row_grads, gate_prob, live_counts, gate_weight, up_weight, down_weight):
    results = exchange(
        row_inputs, row_grads, gate_prob, live_counts, gate_weight.T, up_weight.T, down_weight, blocks
    )
    gate_t, up_t, down_grad, input_grad, prob_grad = hand_over(*results, row_inputs.shape[0] // 8)
    return (input_grad, prob_grad, gate_t.T, up_t.T, down_grad)


def solution(mesh, blocks=(1024, 1024)):
    return jax.shard_map(
        functools.partial(shards, blocks),
        mesh=mesh,
        in_specs=(
            P("blk", None),
            P("blk", None),
            P("blk"),
            P("blk"),
            P(None, ("blk", "seq")),
            P(None, ("blk", "seq")),
            P(("blk", "seq"), None),
        ),
        out_specs=(
            P(("blk", "seq"), None),
            P(("blk", "seq")),
            P(None, ("blk", "seq")),
            P(None, ("blk", "seq")),
            P(("blk", "seq"), None),
        ),
        check_vma=False,
    )
```

time: 790 us -> 115 us (0.15)
  waiting for transfers between devices: 462 us -> 0 us
  matrix products: 162 us -> 0 us
  Pallas kernels: 0 us -> 113 us
  local copies, waits for them, and re-layouts: 99.8 us -> 0 us
  blocking collectives: 24.6 us -> 0 us
  other arithmetic: 21.1 us -> 0 us
  between operations: 15.3 us -> 1.47 us
    ppermute x15 -> x0, waiting for transfers between devices: 259 us -> none  [shifted(): lax.ppermute(value, axis, [(i, (i + by) % count) for i in range(count)])]
    reduce_scatter x3 -> x0, waiting for transfers between devices: 203 us -> none  [the longest x1 81.7 us: shards(): lax.psum_scatter(input_total.astype(jnp.bfloat16), 'seq', scatter_dimensi...]
    dot_general x80 -> x0, matrix products: 162 us -> none  [the longest x32 46.4 us: contract_rows(): lax.dot_general(left, right, (((0,), (0,)), ((), ())), preferred_element_...]
    pallas_call x0 -> x2, Pallas kernels: none -> 113 us  [the longest x1 111 us: exchange(): pl.pallas_call(functools.partial(kernel, units=units, rows=rows, feats=fe...]
    while x165 -> x0, local copies, waits for them, and re-layouts: 84 us -> none
    unnamed x1 -> x0, blocking collectives: 24.6 us -> none
    convert_element_type x20 -> x0, other arithmetic: 18.5 us -> none  [the longest x16 12 us: shards(): (jnp.arange(row_count, dtype=jnp.int32) < live_count).astype(jnp.float32)]
  transfers between devices with their start and end apart: 18 -> 0, of which waited for: 18 -> 0; matrix products, arithmetic and copies ran while one was open for 3% -> 0% of each run, Pallas kernels for 0% -> 0%
where the time goes in v2:
time: 115 us
  Pallas kernels  113 us (98%)
  between operations  1.47 us (1%)
    pallas_call x1, Pallas kernels, exchange(): pl.pallas_call(functools.partial(kernel, units=units, rows=rows, feats=fe...  111 us

profile of v2, /device:TPU:32, one launch (start us, length us, event | category | flops | bytes accessed | tf_op | source)
XLA Modules:
  0.0 114.6 jit_solution(10835657945014149284)
XLA Ops:
  1.3 111.5 %exchange.1 = (bf16[64,3072]{1,0:T(8,128)(2,1)S(1)}, bf16[64,3072]{1,0:T(8,128)(2,1)S(1)}, bf16[64,3072]{1,0:T(8,128)(2,1)S(1)}, bf16[64,3072]{1,0:T(8,128)(2,1)S(1)}, f32[8,128]{1,0:T(8,128)S(1)}) custom-call(bf16[512,3072]{1,0:T(8,128)(2,1)} %x_hbm.1, bf16[512,3072]{1,0:T(8,128)(2,1)} %g_hbm.1, f32[4,128]{1,0:T(4,128)} %bitcast.9, s32[1]{0:T(128)S(6)} %copy.12.count_hbm, ...), custom_call_target="tpu_custom_call" | custom-call | flops 25769803776 | bytes 37748736 | tf_op jit(solution)/shard_map/exchange/pallas_call | solution.py:434
  112.8 1.7 %hand_over.1 = (bf16[64,3072]{1,0:T(8,128)(2,1)}, bf16[64,3072]{1,0:T(8,128)(2,1)}, bf16[64,3072]{1,0:T(8,128)(2,1)}, bf16[64,3072]{1,0:T(8,128)(2,1)}, f32[64]{0:T(128)}) custom-call(bf16[64,3072]{1,0:T(8,128)(2,1)S(1)} %get-tuple-element.15.gate_in, bf16[64,3072]{1,0:T(8,128)(2,1)S(1)} %get-tuple-element.16.up_in, ...), custom_call_target="tpu_custom_call" | custom-call | tf_op jit(solution)/shard_map/hand_over/pallas_call | solution.py:489

commit v3 on v2

--- a/solution.py
+++ b/solution.py
@@ -22,14 +22,16 @@
 L2, Z2 = (3, 0), (3, 1)
 CHUNKS = range(6)
 TURN = (1, 1, 1, -1, -1, -1)
-ALONG_X = (0, 1, 4, 5)
+GO_ALONG_X = (0, 1, 2, 3, 4, 5)
+BACK_ALONG_X = (0, 5)
+LAG = 60
 ORDER = (
-    63, 61, 45, 48, 15, 46, 60, 1, 90, 64, 3, 62, 76, 18, 31, 47, 49, 33, 16, 2, 4, 19, 77, 65, 78, 6, 50, 80, 34,
-    21, 35, 32, 81, 5, 66, 79, 17, 95, 96, 98, 0, 75, 30, 20, 97, 100, 99, 51, 101, 23, 102, 53, 36, 91, 55, 92, 68,
-    93, 94, 52, 54, 24, 104, 103, 69, 106, 71, 115, 38, 70, 105, 26, 107, 67, 108, 25, 116, 41, 118, 56, 8, 109, 86,
-    85, 111, 112, 117, 132, 124, 40, 42, 10, 110, 131, 125, 119, 27, 113, 22, 72, 120, 82, 57, 122, 133, 114, 83, 9,
-    11, 28, 121, 134, 58, 127, 128, 37, 136, 12, 43, 123, 129, 135, 73, 84, 39, 87, 13, 7, 126, 29, 137, 59, 88,
-    130, 74, 44, 14, 89, 138,
+    18, 31, 75, 76, 63, 45, 90, 15, 61, 46, 16, 1, 0, 30, 32, 3, 60, 78, 19, 48, 33, 64, 4, 91, 47, 62, 21, 92, 5,
+    79, 77, 65, 93, 49, 34, 96, 66, 2, 95, 98, 51, 6, 80, 109, 17, 97, 36, 111, 94, 82, 37, 20, 81, 22, 35, 100, 50,
+    99, 102, 83, 101, 23, 38, 53, 25, 55, 107, 24, 8, 84, 103, 39, 104, 115, 54, 108, 105, 10, 116, 106, 86, 85, 26,
+    112, 41, 117, 124, 132, 40, 56, 11, 118, 71, 110, 131, 70, 125, 9, 120, 113, 42, 114, 119, 27, 121, 57, 133,
+    134, 68, 136, 135, 129, 122, 12, 52, 72, 43, 128, 126, 28, 87, 7, 58, 67, 73, 69, 127, 44, 123, 137, 59, 88, 13,
+    130, 29, 74, 14, 139, 89, 138, 140,
 )
 
 
@@ -83,6 +85,7 @@
 
     routes = {}
     pending = []
+    now = [0]
     here = set()
 
     def route(name, src, dst, target):
@@ -96,7 +99,7 @@
         for name in names:
             copy = routes[name]()
             copy.start()
-            pending.append(copy)
+            pending.append((now[0], copy))
 
     def need(*names):
         for name in names:
@@ -116,11 +119,13 @@
             route((BACK_L, e, h), chunk(DG, l_at(e), h), RXF.at[side(e), h], along_x(e))
         route((GO_L2, h), chunk(W, l_at(-t), h), chunk(W, L2, h), along_x(t))
         route((BACK_L2, h), chunk(DG, L2, h), RX2.at[h], along_x(t))
-        if h in ALONG_X:
+        if h in GO_ALONG_X:
             route((GO_Z2, h), chunk(W, z_at(-t), h), chunk(W, Z2, h), along_x(t))
-            route((BACK_X2, h), chunk(DG, Z2, h), RZX.at[ALONG_X.index(h)], along_x(t))
         else:
             route((GO_Z2, h), chunk(W, L2, h), chunk(W, Z2, h), z_next)
+        if h in BACK_ALONG_X:
+            route((BACK_X2, h), chunk(DG, Z2, h), RZX.at[BACK_ALONG_X.index(h)], along_x(t))
+        else:
             route((BACK_Z2, h), chunk(DG, Z2, h), RZ.at[3, h], z_back)
 
     mine = pl.ds(pl.multiple_of(c * rows, rows), rows)
@@ -176,13 +181,13 @@
         up_back = weighted * activated
         GB[p, lines, 0 : 2 * U] = gate_back.astype(BF16)
         GB[p, lines, 2 * U :] = up_back.astype(BF16)
-        AT[:, lines] = jnp.concatenate([gate_back, up_back, weight * hidden], axis=1).T.astype(BF16)
+        AT[p, :, lines] = jnp.concatenate([gate_back, up_back, weight * hidden], axis=1).T.astype(BF16)
 
     def weight_terms(p, first, last, rows_ref):
         def body(i, carry):
             cols = pl.ds(pl.multiple_of(i * nb_dw, nb_dw), nb_dw)
             DG[p, first:last, cols] = lax.dot_general(
-                AT[first:last, :], rows_ref[:, cols], NN, preferred_element_type=F32
+                AT[p, first:last, :], rows_ref[:, cols], NN, preferred_element_type=F32
             ).astype(BF16)
             return carry
 
@@ -266,15 +271,15 @@
             hand_on((), (GO_L, e, h))
             hand_on(((GO_L, e, h),), (GO_Z, e, h))
         hand_on(((GO_L, -t, h),), (GO_L2, h))
-        hand_on(((GO_Z, -t, h) if h in ALONG_X else (GO_L2, h),), (GO_Z2, h))
+        hand_on(((GO_Z, -t, h) if h in GO_ALONG_X else (GO_L2, h),), (GO_Z2, h))
         hand_on((), (BACK_Z0, h))
         hand_on((), (BACK_Z, -t, h))
         add_on(((BACK_Z, -t, h),), chunk(DG, l_at(-t), h), (RZ.at[1 + side(-t), h],), (BACK_L, -t, h)
         )
-        if h in ALONG_X:
+        if h in BACK_ALONG_X:
             hand_on((), (BACK_X2, h))
             hand_on((), (BACK_L2, h))
-            add_on(((BACK_X2, h),), chunk(DG, z_at(t), h), (RZX.at[ALONG_X.index(h)],), (BACK_Z, t, h)
+            add_on(((BACK_X2, h),), chunk(DG, z_at(t), h), (RZX.at[BACK_ALONG_X.index(h)],), (BACK_Z, t, h)
             )
         else:
             hand_on((), (BACK_Z, t, h))
@@ -381,10 +386,16 @@
                 add_to(halves(IG.at[0, 3, h])[q], halves(YF.at[0, h])[q], halves(YF.at[1, h])[q])
             send((FAR_Z, q))
 
+    for q in range(2):
+
+        @tasks.append
+        def _(q=q):
+            need((FAR_Z, q))
+            add_into(halves(in_out)[q], halves(IG.at[0, 3, zh])[q], halves(ZF)[q])
+
     @tasks.append
     def _():
-        need((FAR_Z, PROB), (FAR_Z, 0), (FAR_Z, 1))
-        add_into(in_out, IG.at[0, 3, zh], ZF)
+        need((FAR_Z, PROB))
         lane = lax.broadcasted_iota(jnp.int32, (8, 128), 1)
         prob_out[...] = jnp.where(seq * part + lane < count_ref[0], PB[0, 3, zh] + PZ[...], 0.0)
 
@@ -399,9 +410,12 @@
     PB[...] = jnp.zeros_like(PB)
     pl.semaphore_wait(barrier, len(friends))
     assert sorted(ORDER) == list(range(len(tasks)))
-    for number in ORDER:
+    for place, number in enumerate(ORDER):
+        now[0] = place
         tasks[number]()
-    for copy in pending:
+        while pending and pending[0][0] < place - LAG:
+            pending.pop(0)[1].wait_send()
+    for _, copy in pending:
         copy.wait_send()
 
 
@@ -448,11 +462,11 @@
             held(2 * rows, 128, kind=F32),
             held(4, 6 * units, feats),
             held(4, 2 * rows, 4 * units),
-            held(6 * units, 2 * rows),
+            held(4, 6 * units, 2 * rows),
             held(2 * rows, 2 * units, kind=F32),
             held(4, 6 * units, feats),
             held(4, 6, units // 2, feats),
-            held(len(ALONG_X), units // 2, feats),
+            held(len(BACK_ALONG_X), units // 2, feats),
             held(6, units // 2, feats),
             held(2, 6, units // 2, feats),
             held(2, 4, 2, *slab),

time: 115 us -> 112 us (0.974)
  Pallas kernels: 113 us -> 110 us
    pallas_call x1, Pallas kernels: 111 us -> 109 us  [exchange(): pl.pallas_call(functools.partial(kernel, units=units, rows=rows, feats=fe...]
where the time goes in v3:
time: 112 us
  Pallas kernels  110 us (98%)
  between operations  1.47 us (1%)
    pallas_call x1, Pallas kernels, exchange(): pl.pallas_call(functools.partial(kernel, units=units, rows=rows, feats=fe...  109 us

profile of v3, /device:TPU:32, one launch (start us, length us, event | category | flops | bytes accessed | tf_op | source)
XLA Modules:
  0.0 111.9 jit_solution(1178368690601852826)
XLA Ops:
  1.3 108.8 %exchange.1 = (bf16[64,3072]{1,0:T(8,128)(2,1)S(1)}, bf16[64,3072]{1,0:T(8,128)(2,1)S(1)}, bf16[64,3072]{1,0:T(8,128)(2,1)S(1)}, bf16[64,3072]{1,0:T(8,128)(2,1)S(1)}, f32[8,128]{1,0:T(8,128)S(1)}) custom-call(bf16[512,3072]{1,0:T(8,128)(2,1)} %x_hbm.1, bf16[512,3072]{1,0:T(8,128)(2,1)} %g_hbm.1, f32[4,128]{1,0:T(4,128)} %bitcast.9, s32[1]{0:T(128)S(6)} %copy.12.count_hbm, ...), custom_call_target="tpu_custom_call" | custom-call | flops 25769803776 | bytes 37748736 | tf_op jit(solution)/shard_map/exchange/pallas_call | solution.py:448
  110.0 1.7 %hand_over.1 = (bf16[64,3072]{1,0:T(8,128)(2,1)}, bf16[64,3072]{1,0:T(8,128)(2,1)}, bf16[64,3072]{1,0:T(8,128)(2,1)}, bf16[64,3072]{1,0:T(8,128)(2,1)}, f32[64]{0:T(128)}) custom-call(bf16[64,3072]{1,0:T(8,128)(2,1)S(1)} %get-tuple-element.15.gate_in, bf16[64,3072]{1,0:T(8,128)(2,1)S(1)} %get-tuple-element.16.up_in, ...), custom_call_target="tpu_custom_call" | custom-call | tf_op jit(solution)/shard_map/hand_over/pallas_call | solution.py:503

commit v4 on v3

--- a/solution.py
+++ b/solution.py
@@ -421,7 +421,12 @@
 
 def finish(gate_in, up_in, down_in, rows_in, prob_in, gate_out, up_out, down_out, rows_out, prob_out, sems):
     pairs = ((gate_in, gate_out), (up_in, up_out), (down_in, down_out), (rows_in, rows_out))
-    copies = [pltpu.make_async_copy(src, dst, sems.at[n]) for n, (src, dst) in enumerate(pairs)]
+    half = gate_in.shape[0] // 2
+    copies = [
+        pltpu.make_async_copy(src.at[pl.ds(q * half, half), :], dst.at[pl.ds(q * half, half), :], sems.at[2 * n + q])
+        for n, (src, dst) in enumerate(pairs)
+        for q in range(2)
+    ]
     for copy in copies:
         copy.start()
     prob_out[...] = prob_in[0, 0 : prob_out.shape[0]]
@@ -506,7 +511,7 @@
         + (jax.ShapeDtypeStruct((part,), F32),),
         in_specs=[vmem] * 5,
         out_specs=(any_space,) * 4 + (vmem,),
-        scratch_shapes=[pltpu.SemaphoreType.DMA((4,))],
+        scratch_shapes=[pltpu.SemaphoreType.DMA((8,))],
         name="hand_over",
     )(*(pltpu.with_memory_space_constraint(a, pltpu.VMEM) for a in (*arrays, prob)))
 

time: 112 us -> 112 us (level)
  no operation moved by 1% of the time
where the time goes in v4:
time: 112 us
  Pallas kernels  110 us (98%)
  between operations  1.47 us (1%)
    pallas_call x1, Pallas kernels, exchange(): pl.pallas_call(functools.partial(kernel, units=units, rows=rows, feats=fe...  109 us

profile of v4, /device:TPU:32, one launch (start us, length us, event | category | flops | bytes accessed | tf_op | source)
XLA Modules:
  0.0 111.9 jit_solution(15551238952047900747)
XLA Ops:
  1.3 108.8 %exchange.1 = (bf16[64,3072]{1,0:T(8,128)(2,1)S(1)}, bf16[64,3072]{1,0:T(8,128)(2,1)S(1)}, bf16[64,3072]{1,0:T(8,128)(2,1)S(1)}, bf16[64,3072]{1,0:T(8,128)(2,1)S(1)}, f32[8,128]{1,0:T(8,128)S(1)}) custom-call(bf16[512,3072]{1,0:T(8,128)(2,1)} %x_hbm.1, bf16[512,3072]{1,0:T(8,128)(2,1)} %g_hbm.1, f32[4,128]{1,0:T(4,128)} %bitcast.9, s32[1]{0:T(128)S(6)} %copy.12.count_hbm, ...), custom_call_target="tpu_custom_call" | custom-call | flops 25769803776 | bytes 37748736 | tf_op jit(solution)/shard_map/exchange/pallas_call | solution.py:453
  110.0 1.7 %hand_over.1 = (bf16[64,3072]{1,0:T(8,128)(2,1)}, bf16[64,3072]{1,0:T(8,128)(2,1)}, bf16[64,3072]{1,0:T(8,128)(2,1)}, bf16[64,3072]{1,0:T(8,128)(2,1)}, f32[64]{0:T(128)}) custom-call(bf16[64,3072]{1,0:T(8,128)(2,1)S(1)} %get-tuple-element.15.gate_in, bf16[64,3072]{1,0:T(8,128)(2,1)S(1)} %get-tuple-element.16.up_in, ...), custom_call_target="tpu_custom_call" | custom-call | tf_op jit(solution)/shard_map/hand_over/pallas_call | solution.py:508
